TPU v7x, 32 devices: a whole 2x2x4 slice. The times are simulated.
32 devices in a mesh: occ: 8 (over y, x, core), vir: 4 (over z).
Axes of the slice: x: 2, y: 2, z: 4, core: 2. Of those that a mesh axis runs over, the one named last changes fastest.
Arguments:
- amplitudes: bfloat16 [1600, 2560], P('occ', 'vir'), may hold values from -6 to 6
- ladder_ints: bfloat16 [2560, 2560], P('vir', 'occ'), may hold values from -0.15625 to 0.15625
- cycle_ints: bfloat16 [2560, 2560], P('vir', 'occ'), may hold values from -0.15625 to 0.15625
- screen: int32 [40, 40], P('occ', 'vir'), may hold values 0 or 1
Outputs:
- residual: bfloat16 [1600, 2560], P('occ', 'vir')
All inputs are finite; a program needn't handle non-finite values. No bound on the sum of `screen` on one device may be relied on, other than what follows from the above.
Results may differ from a plain program's by a relative error of at most 0.0044.
Values may be sent and summed in bfloat16 or wider, within the bound.
A program may use at most 128 MiB of HBM per device.

v0:
```python
import jax
import jax.numpy as jnp
from jax import lax
from jax.sharding import PartitionSpec as P


def shards(amplitudes, ladder_ints, cycle_ints, screen):
    orbital_rows, tile_count = screen.shape
    occupied = amplitudes.shape[0] // orbital_rows
    columns = amplitudes.shape[1]
    tile_width = columns // tile_count
    groups = lax.axis_size("occ")
    values = screen.astype(jnp.float32)
    keep = jnp.broadcast_to(
        values[:, None, :, None], (orbital_rows, occupied, tile_count, tile_width)
    )
    keep = keep.reshape(orbital_rows * occupied, columns)
    masked = (amplitudes.astype(jnp.float32) * keep).astype(jnp.bfloat16)
    blocks = masked.reshape(orbital_rows, groups, orbital_rows, columns)
    arrived = lax.all_to_all(blocks, "occ", split_axis=1, concat_axis=1, tiled=True)
    swapped = arrived.transpose(2, 1, 0, 3).reshape(orbital_rows * occupied, columns)
    cycle_input = (2.0 * masked.astype(jnp.float32) - swapped.astype(jnp.float32)).astype(
        jnp.bfloat16
    )
    ladder = None
    cycle_part = jnp.dot(
        cycle_input,
        lax.all_gather(cycle_ints, "occ", axis=1, tiled=True),
        preferred_element_type=jnp.float32,
    )
    ladder = jnp.dot(
        masked,
        lax.all_gather(ladder_ints, "occ", axis=1, tiled=True),
        preferred_element_type=jnp.float32,
    )
    summed = lax.psum_scatter(ladder + cycle_part, "vir", scatter_dimension=1, tiled=True)
    return (keep * summed).astype(jnp.bfloat16)


def solution(mesh):
    placed = (P("occ", "vir"), P("vir", "occ"), P("vir", "occ"), P("occ", "vir"))
    return jax.shard_map(
        shards, mesh=mesh, in_specs=placed, out_specs=P("occ", "vir"), check_vma=False
    )
```

profile of v0, /device:TPU:0, one launch (start us, length us, event | category | flops | bytes accessed | tf_op | source)
XLA Modules:
  0.0 135.9 jit_solution(16828011823220860868)
XLA Ops:
  6.5 0.0 copy-start
  6.5 0.0 all-gather.3.cloned.1.call-start
  6.5 0.7 all-gather.3.cloned.1.call-update
  7.3 0.0 all-gather.5.cloned.1.call-start
  7.3 0.7 all-gather.5.cloned.1.call-update
  8.0 0.0 reduce-scatter.2.cloned.1.call-start
  8.1 0.7 convert_element_type.27
  8.7 0.2 broadcast_in_dim.2
  8.9 0.4 reshape.10
  9.3 0.0 copy-done
  9.3 0.1 multiply_convert_fusion.1
  9.4 0.1 reshape.11
  9.5 13.5 %all_to_all.5 = bf16[5,8,5,640]{3,2,0,1:T(8,128)(2,1)S(1)} all-to-all(bf16[5,8,5,640]{3,2,0,1:T(8,128)(2,1)S(1)} %copy.7), channel_id=1, replica_groups=mesh['occ'=8,'vir'=4] {'occ'}, dimensions={1} | all-to-all | bytes 512000 | tf_op jit(solution)/shard_map/all_to_all | solution.py:20
  23.0 0.1 convert_bitcast_fusion
  23.1 0.2 copy.8
  23.3 0.1 reshape.12
  23.4 21.6 %all-gather.3.cloned.1.call-done = bf16[640,2560]{0,1:T(8,128)(2,1)} async-done(((bf16[640,320]{0,1:T(8,128)(2,1)}), bf16[640,2560]{0,1:T(8,128)(2,1)}) %all-gather.3.cloned.1.call-update) | async-done | bytes 3276816 | tf_op jit(solution)/shard_map/all_gather | solution.py:33
  44.9 3.3 %fusion.2 = f32[200,2560]{1,0:T(8,128)S(1)} fusion(bf16[200,640]{1,0:T(8,128)(2,1)S(1)} %multiply_convert_fusion.1, bf16[640,2560]{0,1:T(8,128)(2,1)} %all-gather.3.cloned.1.call-done), kind=kOutput, calls=%fused_computation.7 | convolution fusion | flops 655360000 | bytes 5580800 | tf_op jit(solution)/shard_map/dot_general | solution.py:31
  48.2 31.5 %all-gather.5.cloned.1.call-done = bf16[640,2560]{0,1:T(8,128)(2,1)} async-done(((bf16[640,320]{0,1:T(8,128)(2,1)}), bf16[640,2560]{0,1:T(8,128)(2,1)}) %all-gather.5.cloned.1.call-update) | async-done | bytes 3276816 | tf_op jit(solution)/shard_map/all_gather | solution.py:28
  79.7 4.7 %convolution_add_fusion = f32[200,2560]{1,0:T(8,128)} fusion(f32[200,2560]{1,0:T(8,128)S(1)} %fusion.2, bf16[640,2560]{0,1:T(8,128)(2,1)} %all-gather.5.cloned.1.call-done, f32[200,640]{1,0:T(8,128)S(1)} %reshape.12, bf16[200,640]{1,0:T(8,128)(2,1)S(1)} %multiply_convert_fusion.1), kind=kOutput, calls=%fused_computation | convolution fusion | flops 656384000 | bytes 8140800 | tf_op jit(solution)/shard_map/dot_general | solution.py:26
  84.4 0.0 reduce-scatter.2.cloned.1.call-update
  84.5 43.2 %reduce-scatter.2.cloned.1.call-done = f32[200,640]{1,0:T(8,128)} async-done(((f32[200,2560]{1,0:T(8,128)}), f32[200,640]{1,0:T(8,128)}) %reduce-scatter.2.cloned.1.call-update) | async-done | bytes 512016 | tf_op jit(solution)/shard_map/reduce_scatter | solution.py:36
  127.6 1.8 %multiply_convert_fusion = bf16[200,640]{1,0:T(8,128)(2,1)} fusion(f32[200,640]{1,0:T(8,128)S(1)} %reshape.10, f32[200,640]{1,0:T(8,128)} %reduce-scatter.2.cloned.1.call-done), kind=kLoop, calls=%fused_computation.2 | loop fusion | flops 256000 | bytes 1280000 | tf_op jit(solution)/shard_map/convert_element_type | solution.py:37
  (1 shorter events, 0.0 us)
Async XLA Ops:
  6.5 2.8 %copy-start = (bf16[200,640]{1,0:T(8,128)(2,1)S(1)}, bf16[200,640]{1,0:T(8,128)(2,1)}, u32[]{:S(2)}) copy-start(bf16[200,640]{1,0:T(8,128)(2,1)} %param.4) | copy-start | bytes 768004
  6.5 38.4 %all-gather.3.cloned.1.call-start = ((), (), s32[]{:S(2)}) async-start(), calls=%async_computation.2 | async-start | bytes 3686400 | tf_op jit(solution)/shard_map/all_gather | solution.py:33
  7.3 72.5 %all-gather.5.cloned.1.call-start = ((), (), s32[]{:S(2)}) async-start(), calls=%async_computation.3 | async-start | bytes 3686400 | tf_op jit(solution)/shard_map/all_gather | solution.py:28
  8.0 119.6 %reduce-scatter.2.cloned.1.call-start = ((), (), s32[]{:S(2)}) async-start(), calls=%async_computation.4 | async-start | bytes 2560000 | tf_op jit(solution)/shard_map/reduce_scatter | solution.py:36
Sparse Core Ops, SparseCore 0:
  9.2 35.6 all-gather.2
  46.8 32.8 all-gather.4
  84.6 43.0 reduce-scatter.1
where the time goes:
time: 136 us
  waiting for transfers between devices  97.7 us (72%)
  blocking collectives  13.5 us (10%)
  between operations  13.2 us (10%)
  matrix products  7.98 us (6%)
  other arithmetic  2.59 us (2%)
    reduce_scatter x1, waiting for transfers between devices, shards(): lax.psum_scatter(ladder + cycle_part, 'vir', scatter_dimension=1, tiled=T...  43.2 us
    all_gather x1, waiting for transfers between devices, shards(): lax.all_gather(cycle_ints, 'occ', axis=1, tiled=True)  31.5 us
    all_gather x1, waiting for transfers between devices, shards(): lax.all_gather(ladder_ints, 'occ', axis=1, tiled=True)  21.6 us
    all_to_all x1, blocking collectives, shards(): lax.all_to_all(blocks, 'occ', split_axis=1, concat_axis=1, tiled=True)  13.5 us
    dot_general x1, matrix products, shards(): jnp.dot(cycle_input, lax.all_gather(cycle_ints, 'occ', axis=1, tiled=True...  4.69 us
    dot_general x1, matrix products, shards(): jnp.dot(masked, lax.all_gather(ladder_ints, 'occ', axis=1, tiled=True), p...  3.3 us
  transfers between devices with their start and end apart: 3, of which 3 were waited for; matrix products, arithmetic and copies ran while one was open for 4% of the time, Pallas kernels for 0%

commit v1 on v0

v1 whole, which is shorter than its diff:
```python
import functools

import jax
import jax.numpy as jnp
from jax import lax
from jax.experimental import pallas as pl
from jax.experimental.pallas import tpu as pltpu
from jax.sharding import PartitionSpec as P

MESH = pl.DeviceIdType.MESH
LANES = 128
F32, BF16 = jnp.float32, jnp.bfloat16


def plain(amplitudes, ladder_ints, cycle_ints, screen):
    orbital_rows, tile_count = screen.shape
    occupied = amplitudes.shape[0] // orbital_rows
    columns = amplitudes.shape[1]
    tile_width = columns // tile_count
    groups = lax.axis_size("occ")
    values = screen.astype(F32)
    keep = jnp.broadcast_to(
        values[:, None, :, None], (orbital_rows, occupied, tile_count, tile_width)
    )
    keep = keep.reshape(orbital_rows * occupied, columns)
    masked = (amplitudes.astype(F32) * keep).astype(BF16)
    blocks = masked.reshape(orbital_rows, groups, orbital_rows, columns)
    arrived = lax.all_to_all(blocks, "occ", split_axis=1, concat_axis=1, tiled=True)
    swapped = arrived.transpose(2, 1, 0, 3).reshape(orbital_rows * occupied, columns)
    cycle_input = (2.0 * masked.astype(F32) - swapped.astype(F32)).astype(BF16)
    cycle_part = jnp.dot(
        cycle_input,
        lax.all_gather(cycle_ints, "occ", axis=1, tiled=True),
        preferred_element_type=F32,
    )
    ladder = jnp.dot(
        masked,
        lax.all_gather(ladder_ints, "occ", axis=1, tiled=True),
        preferred_element_type=F32,
    )
    summed = lax.psum_scatter(ladder + cycle_part, "vir", scatter_dimension=1, tiled=True)
    return (keep * summed).astype(BF16)


def kernel(
    nv, norb, nocc,
    amp, lad, cyc, scr, out,
    G, G32, I, W, O, R, keep_ref,
    gs, gr, osem, orx,
):
    rows, cols = out.shape
    pad = G.shape[1]
    half = cols // 2
    tile = cols // scr.shape[1]
    cut = (rows // 32) * 16
    o = lax.axis_index("occ")
    z = lax.axis_index("vir")
    k = o % 2
    c = o // 2
    nc = nv
    sib = o + 1 - 2 * k
    cx = c + 1 - 2 * (c % 2)
    cy = c + 2 - 4 * ((c // 2) % 2)
    cd = cx + 2 - 4 * ((cx // 2) % 2)
    X, Y, D = 2 * cx + k, 2 * cy + k, 2 * cd + k
    mine = z == c

    barrier = pltpu.get_barrier_semaphore()
    for p in (sib, X, Y):
        pl.semaphore_signal(barrier, inc=1, device_id={"occ": p, "vir": z}, device_id_type=MESH)
    for q in range(nv):
        src = 2 * z + k

        @pl.when(jnp.logical_not((src == o) & (z == q)))
        def _():
            pl.semaphore_signal(
                barrier, inc=1, device_id={"occ": src, "vir": q}, device_id_type=MESH
            )

    t_of = lax.broadcasted_iota(jnp.int32, (scr.shape[1], cols), 0)
    v_of = lax.broadcasted_iota(jnp.int32, (scr.shape[1], cols), 1)
    spread = ((v_of >= t_of * tile) & (v_of < (t_of + 1) * tile)).astype(F32)
    wide = jnp.dot(scr[...].astype(F32), spread, preferred_element_type=F32)
    r_of = lax.broadcasted_iota(jnp.int32, (rows, norb), 0)
    a_of = lax.broadcasted_iota(jnp.int32, (rows, norb), 1)
    pick = ((r_of >= a_of * nocc) & (r_of < (a_of + 1) * nocc)).astype(F32)
    keep = jnp.dot(pick, wide, preferred_element_type=F32)
    keep_ref[...] = keep
    masked = amp[...].astype(F32) * keep
    masked = jnp.concatenate([masked, jnp.zeros((pad - rows, cols), F32)], axis=0)
    G[o] = masked.astype(BF16)

    pl.semaphore_wait(barrier, jnp.where(mine, 3 + nv - 1, 3 + nv))

    def cp(src, dst, sem, p):
        return pltpu.make_async_remote_copy(
            src_ref=src, dst_ref=dst, send_sem=gs.at[sem], recv_sem=gr.at[sem],
            device_id={"occ": p, "vir": z}, device_id_type=MESH,
        )

    def blk(s, h=None):
        if h is None:
            return G.at[s]
        return G.at[s, pl.ds(0, cut)] if h == 0 else G.at[s, pl.ds(cut, pad - cut)]

    def widen(s):
        val = G[s].astype(F32)[:rows]
        at = pl.multiple_of(s * rows, 8)
        for l in range(cols // LANES):
            G32[l, pl.ds(at, rows), :] = val[:, l * LANES:(l + 1) * LANES]

    sends = []

    def send(s, h, sem, p):
        d = cp(blk(s, h), blk(s, h), sem, p)
        d.start()
        sends.append(d)

    def arrive(s, h, sem):
        cp(blk(s, h), blk(s, h), sem, sib).wait_recv()

    send(o, 0, 0, X)
    send(o, 1, 3, Y)
    send(o, 1, 1, X)
    send(o, 0, 2, Y)
    send(o, None, 6, sib)
    for m, ref in enumerate((lad, cyc)):
        d = cp(ref, I.at[k, m], 10 + m, sib)
        d.start()
        sends.append(d)
        I[k, m] = ref[...]
    widen(o)
    arrive(X, 0, 0)
    send(X, 0, 4, Y)
    arrive(Y, 1, 3)
    send(Y, 1, 5, X)
    arrive(sib, None, 6)
    widen(sib)
    for m in range(2):
        cp(I.at[1 - k, m], I.at[1 - k, m], 10 + m, sib).wait_recv()
        W[m] = jnp.concatenate([I[0, m], I[1, m]], axis=1)
    SX, SY, SD = X + 1 - 2 * k, Y + 1 - 2 * k, D + 1 - 2 * k
    arrive(X, 1, 1)
    send(X, None, 7, sib)
    arrive(Y, 0, 2)
    send(Y, None, 8, sib)
    widen(X)
    widen(Y)
    arrive(SX, None, 7)
    widen(SX)
    arrive(SY, None, 8)
    widen(SY)
    arrive(D, 0, 4)
    arrive(D, 1, 5)
    send(D, None, 9, sib)
    widen(D)
    arrive(SD, None, 9)
    widen(SD)

    def out_copy(t, chip, slot, zz):
        return pltpu.make_async_remote_copy(
            src_ref=O.at[t], dst_ref=R.at[slot], send_sem=osem.at[t], recv_sem=orx.at[slot],
            device_id={"occ": 2 * chip + k, "vir": zz}, device_id_type=MESH,
        )

    def step(t, carry):
        chip = (c + t + 1) % nc
        dest = 2 * chip + k
        m = G[dest]
        parts = []
        for a in range(norb):
            i = dest * norb + a
            parts.append(jnp.concatenate(
                [G32[l, pl.ds(i, nocc, stride=nocc), :] for l in range(cols // LANES)], axis=1))
        parts.append(jnp.zeros((pad - rows, cols), F32))
        swapped = jnp.concatenate(parts, axis=0)
        ci = (2.0 * m.astype(F32) - swapped).astype(BF16)
        acc = jnp.dot(m, W[0], preferred_element_type=F32)
        acc = acc + jnp.dot(ci, W[1], preferred_element_type=F32)
        O[t] = acc.astype(BF16)
        here = (chip == c) & mine

        @pl.when(jnp.logical_not(here))
        def _():
            out_copy(t, chip, z, c).start()

        return carry

    lax.fori_loop(0, nc, step, 0)

    total = None
    for q in range(nv):
        own = mine & (z == q)

        @pl.when(own)
        def _():
            R[q] = O[nc - 1]

        @pl.when(jnp.logical_not(own))
        def _():
            out_copy(0, c, q, z).wait_recv()

        part = R[q].astype(F32)[:rows]
        total = part if total is None else total + part
    out[...] = (keep_ref[...] * total).astype(BF16)

    for d in sends:
        d.wait_send()
    for t in range(nc):
        if t < nc - 1:
            out_copy(t, c, z, c).wait_send()
        else:
            @pl.when(jnp.logical_not(mine))
            def _():
                out_copy(t, c, z, c).wait_send()


def fused(amplitudes, ladder_ints, cycle_ints, screen):
    norb, tiles = screen.shape
    rows, cols = amplitudes.shape
    nocc = rows // norb
    nv = lax.axis_size("vir")
    groups = lax.axis_size("occ")
    pad = -(-rows // 16) * 16
    vmem = pl.BlockSpec(memory_space=pltpu.VMEM)
    return pl.pallas_call(
        functools.partial(kernel, nv, norb, nocc),
        out_shape=jax.ShapeDtypeStruct((rows, cols), BF16),
        in_specs=[vmem] * 4,
        out_specs=vmem,
        scratch_shapes=[
            pltpu.VMEM((groups, pad, cols), BF16),
            pltpu.VMEM((cols // LANES, groups * rows, LANES), F32),
            pltpu.VMEM((2, 2) + ladder_ints.shape, BF16),
            pltpu.VMEM((2, cols, cols), BF16),
            pltpu.VMEM((nv, pad, cols), BF16),
            pltpu.VMEM((nv, pad, cols), BF16),
            pltpu.VMEM((rows, cols), F32),
            pltpu.SemaphoreType.DMA((12,)),
            pltpu.SemaphoreType.DMA((12,)),
            pltpu.SemaphoreType.DMA((nv,)),
            pltpu.SemaphoreType.DMA((nv,)),
        ],
        compiler_params=pltpu.CompilerParams(
            collective_id=0, has_side_effects=True, vmem_limit_bytes=48 * 2**20
        ),
    )(amplitudes, ladder_ints, cycle_ints, screen)


def shards(amplitudes, ladder_ints, cycle_ints, screen):
    groups, planes = lax.axis_size("occ"), lax.axis_size("vir")
    rows, cols = amplitudes.shape
    fits = (
        groups == 2 * planes
        and planes == 4
        and cols == 2 * ladder_ints.shape[1]
        and cols == ladder_ints.shape[0]
        and cols % LANES == 0
        and (rows // screen.shape[0]) % 8 == 0
        and groups * rows * cols * 6 < 24 * 2**20
    )
    return (fused if fits else plain)(amplitudes, ladder_ints, cycle_ints, screen)


def solution(mesh):
    placed = (P("occ", "vir"), P("vir", "occ"), P("vir", "occ"), P("occ", "vir"))
    return jax.shard_map(
        shards, mesh=mesh, in_specs=placed, out_specs=P("occ", "vir"), check_vma=False
    )
```

time: 136 us -> 91.1 us (0.67)
  waiting for transfers between devices: 97.7 us -> 0 us
  Pallas kernels: 0 us -> 88 us
  blocking collectives: 13.5 us -> 0 us
  between operations: 13.2 us -> 0.04 us
  matrix products: 7.98 us -> 0 us
  other arithmetic: 2.59 us -> 0 us
  local copies, waits for them, and re-layouts: 0.95 us -> 2.94 us
    pallas_call x0 -> x1, Pallas kernels: none -> 88 us  [fused(): pl.pallas_call(functools.partial(kernel, nv, norb, nocc), out_shape=jax.S...]
    all_gather x2 -> x0, waiting for transfers between devices: 53.1 us -> none  [the longest x1 31.5 us: shards(): lax.all_gather(cycle_ints, 'occ', axis=1, tiled=True)]
    reduce_scatter x1 -> x0, waiting for transfers between devices: 43.2 us -> none  [shards(): lax.psum_scatter(ladder + cycle_part, 'vir', scatter_dimension=1, tiled=T...]
    all_to_all x1 -> x0, blocking collectives: 13.5 us -> none  [shards(): lax.all_to_all(blocks, 'occ', split_axis=1, concat_axis=1, tiled=True)]
    dot_general x2 -> x0, matrix products: 7.98 us -> none  [the longest x1 4.69 us: shards(): jnp.dot(cycle_input, lax.all_gather(cycle_ints, 'occ', axis=1, tiled=True...]
    unnamed x2 -> x9, local copies, waits for them, and re-layouts: 0.01 us -> 2.94 us
    convert_element_type x4 -> x0, other arithmetic: 2.59 us -> none  [the longest x1 1.78 us: shards(): return (keep * summed).astype(jnp.bfloat16)]
    unnamed x3 -> x0, waiting for transfers between devices: 1.42 us -> none
  transfers between devices with their start and end apart: 3 -> 0, of which waited for: 3 -> 0; matrix products, arithmetic and copies ran while one was open for 4% -> 0% of each run, Pallas kernels for 0% -> 0%
where the time goes in v1:
time: 91.1 us; the launch traced here: 91 us
  Pallas kernels  88 us (97%)
  local copies, waits for them, and re-layouts  2.94 us (3%)
    pallas_call x1, Pallas kernels, fused(): pl.pallas_call(functools.partial(kernel, nv, norb, nocc), out_shape=jax.S...  88 us
    unnamed x9, local copies, waits for them, and re-layouts  2.94 us

profile of v1, /device:TPU:0, one launch (start us, length us, event | category | flops | bytes accessed | tf_op | source)
XLA Modules:
  0.0 91.0 jit_solution(8721728128391129353)
XLA Ops:
  0.0 0.0 copy-start.2
  0.0 1.3 %copy.5.lad = bf16[640,320]{1,0:T(8,128)(2,1)S(1)} copy(bf16[640,320]{0,1:T(8,128)(2,1)} %param.5) | data formatting | bytes 819200 | tf_op args[1]
  1.3 0.0 copy-done.2
  1.3 0.0 copy-start
  1.3 0.0 copy-start.1
  1.4 0.3 copy.6.cyc
  1.6 0.7 copy-done
  2.3 0.0 copy-done.1
  2.3 88.0 %shard_map.46 = bf16[200,640]{1,0:T(8,128)(2,1)S(1)} custom-call(bf16[200,640]{1,0:T(8,128)(2,1)S(1)} %copy-done, bf16[640,320]{1,0:T(8,128)(2,1)S(1)} %copy.5.lad, bf16[640,320]{1,0:T(8,128)(2,1)S(1)} %copy.6.cyc, s32[5,10]{1,0:T(8,128)S(1)} %copy-done.1), custom_call_target="tpu_custom_call" | custom-call | tf_op jit(solution)/shard_map/pallas_call | solution.py:226
  90.3 0.7 copy.8
Async XLA Ops:
  0.0 1.3 %copy-start.2 = (bf16[640,320]{0,1:T(8,128)(2,1)S(1)}, bf16[640,320]{0,1:T(8,128)(2,1)}, u32[]{:S(2)}) copy-start(bf16[640,320]{0,1:T(8,128)(2,1)} %param.6) | copy-start | bytes 1228804
  1.3 1.0 %copy-start = (bf16[200,640]{1,0:T(8,128)(2,1)S(1)}, bf16[200,640]{1,0:T(8,128)(2,1)}, u32[]{:S(2)}) copy-start(bf16[200,640]{1,0:T(8,128)(2,1)} %amp.1) | copy-start | bytes 768004
  1.3 0.9 %copy-start.1 = (s32[5,10]{1,0:T(8,128)S(1)}, s32[5,10]{1,0:T(8,128)}, u32[]{:S(2)}) copy-start(s32[5,10]{1,0:T(8,128)} %scr.1) | copy-start | bytes 604

commit v2 on v1

--- a/solution.py
+++ b/solution.py
@@ -45,8 +45,8 @@
 def kernel(
     nv, norb, nocc,
     amp, lad, cyc, scr, out,
-    G, G32, I, W, O, R, keep_ref,
-    gs, gr, osem, orx,
+    G, G32, I, W, O, T, R, keep_ref,
+    gs, gr, osem, orx, lsem, lrx,
 ):
     rows, cols = out.shape
     pad = G.shape[1]
@@ -63,18 +63,16 @@
     cy = c + 2 - 4 * ((c // 2) % 2)
     cd = cx + 2 - 4 * ((cx // 2) % 2)
     X, Y, D = 2 * cx + k, 2 * cy + k, 2 * cd + k
-    mine = z == c
 
     barrier = pltpu.get_barrier_semaphore()
-    for p in (sib, X, Y):
+    for p in (sib, X, Y, D):
         pl.semaphore_signal(barrier, inc=1, device_id={"occ": p, "vir": z}, device_id_type=MESH)
-    for q in range(nv):
-        src = 2 * z + k
-
-        @pl.when(jnp.logical_not((src == o) & (z == q)))
+    for there, ok in ((z - 1, z > 0), (z + 1, z < nv - 1)):
+
+        @pl.when(ok)
         def _():
             pl.semaphore_signal(
-                barrier, inc=1, device_id={"occ": src, "vir": q}, device_id_type=MESH
+                barrier, inc=1, device_id={"occ": o, "vir": there}, device_id_type=MESH
             )
 
     t_of = lax.broadcasted_iota(jnp.int32, (scr.shape[1], cols), 0)
@@ -90,7 +88,7 @@
     masked = jnp.concatenate([masked, jnp.zeros((pad - rows, cols), F32)], axis=0)
     G[o] = masked.astype(BF16)
 
-    pl.semaphore_wait(barrier, jnp.where(mine, 3 + nv - 1, 3 + nv))
+    pl.semaphore_wait(barrier, jnp.where((z == 0) | (z == nv - 1), 5, 6))
 
     def cp(src, dst, sem, p):
         return pltpu.make_async_remote_copy(
@@ -157,10 +155,10 @@
     arrive(SD, None, 9)
     widen(SD)
 
-    def out_copy(t, chip, slot, zz):
+    def out_copy(t, chip, slot):
         return pltpu.make_async_remote_copy(
-            src_ref=O.at[t], dst_ref=R.at[slot], send_sem=osem.at[t], recv_sem=orx.at[slot],
-            device_id={"occ": 2 * chip + k, "vir": zz}, device_id_type=MESH,
+            src_ref=O.at[t], dst_ref=T.at[slot], send_sem=osem.at[t], recv_sem=orx.at[slot],
+            device_id={"occ": 2 * chip + k, "vir": z}, device_id_type=MESH,
         )
 
     def step(t, carry):
@@ -177,42 +175,68 @@
         ci = (2.0 * m.astype(F32) - swapped).astype(BF16)
         acc = jnp.dot(m, W[0], preferred_element_type=F32)
         acc = acc + jnp.dot(ci, W[1], preferred_element_type=F32)
-        O[t] = acc.astype(BF16)
-        here = (chip == c) & mine
-
-        @pl.when(jnp.logical_not(here))
-        def _():
-            out_copy(t, chip, z, c).start()
+        acc = acc.astype(BF16)
+
+        @pl.when(t == nc - 1)
+        def _():
+            T[c] = acc
+
+        @pl.when(t < nc - 1)
+        def _():
+            O[t] = acc
+            out_copy(t, chip, c).start()
 
         return carry
 
     lax.fori_loop(0, nc, step, 0)
 
-    total = None
-    for q in range(nv):
-        own = mine & (z == q)
-
-        @pl.when(own)
-        def _():
-            R[q] = O[nc - 1]
-
-        @pl.when(jnp.logical_not(own))
-        def _():
-            out_copy(0, c, q, z).wait_recv()
-
-        part = R[q].astype(F32)[:rows]
-        total = part if total is None else total + part
-    out[...] = (keep_ref[...] * total).astype(BF16)
+    def line_copy(src, way, tile_at, there):
+        return pltpu.make_async_remote_copy(
+            src_ref=src, dst_ref=R.at[way, tile_at],
+            send_sem=lsem.at[way, tile_at], recv_sem=lrx.at[way, tile_at],
+            device_id={"occ": o, "vir": there}, device_id_type=MESH,
+        )
+
+    def plane_wait(at):
+        @pl.when(c != at)
+        def _():
+            out_copy(0, c, at).wait_recv()
+
+    for zz in range(nv):
+
+        @pl.when(z == zz)
+        def _():
+            ups = [(q, 0) for q in range(nv - 1, zz, -1)]
+            downs = [(q, 1) for q in range(zz)]
+            order = ups + downs if 2 * zz < nv else downs + ups
+            started = []
+            for q, way in order:
+                there = zz + 1 if way == 0 else zz - 1
+                first = zz == 0 if way == 0 else zz == nv - 1
+                plane_wait(q)
+                if first:
+                    src = T.at[q]
+                else:
+                    src = R.at[way, q]
+                    line_copy(src, way, q, there).wait_recv()
+                    R[way, q] = (R[way, q].astype(F32) + T[q].astype(F32)).astype(BF16)
+                d = line_copy(src, way, q, there)
+                d.start()
+                started.append(d)
+            plane_wait(zz)
+            total = T[zz].astype(F32)
+            for way, any_in in ((0, zz > 0), (1, zz < nv - 1)):
+                if any_in:
+                    line_copy(R.at[way, zz], way, zz, zz + 1 if zz == 0 else zz - 1).wait_recv()
+                    total = total + R[way, zz].astype(F32)
+            out[...] = (keep_ref[...] * total[:rows]).astype(BF16)
+            for d in started:
+                d.wait_send()
 
     for d in sends:
         d.wait_send()
-    for t in range(nc):
-        if t < nc - 1:
-            out_copy(t, c, z, c).wait_send()
-        else:
-            @pl.when(jnp.logical_not(mine))
-            def _():
-                out_copy(t, c, z, c).wait_send()
+    for t in range(nc - 1):
+        out_copy(t, c, c).wait_send()
 
 
 def fused(amplitudes, ladder_ints, cycle_ints, screen):
@@ -233,13 +257,16 @@
             pltpu.VMEM((cols // LANES, groups * rows, LANES), F32),
             pltpu.VMEM((2, 2) + ladder_ints.shape, BF16),
             pltpu.VMEM((2, cols, cols), BF16),
+            pltpu.VMEM((nv - 1, pad, cols), BF16),
             pltpu.VMEM((nv, pad, cols), BF16),
-            pltpu.VMEM((nv, pad, cols), BF16),
+            pltpu.VMEM((2, nv, pad, cols), BF16),
             pltpu.VMEM((rows, cols), F32),
             pltpu.SemaphoreType.DMA((12,)),
             pltpu.SemaphoreType.DMA((12,)),
+            pltpu.SemaphoreType.DMA((nv - 1,)),
             pltpu.SemaphoreType.DMA((nv,)),
-            pltpu.SemaphoreType.DMA((nv,)),
+            pltpu.SemaphoreType.DMA((2, nv)),
+            pltpu.SemaphoreType.DMA((2, nv)),
         ],
         compiler_params=pltpu.CompilerParams(
             collective_id=0, has_side_effects=True, vmem_limit_bytes=48 * 2**20

time: 91.1 us -> 53.5 us (0.59)
  the two profiles are of different devices: /device:TPU:0 before, /device:TPU:4 now
where the time goes in v2:
time: 53.5 us; the launch traced here: 53.4 us
  Pallas kernels  50.4 us (94%)
  local copies, waits for them, and re-layouts  2.94 us (5%)
    pallas_call x1, Pallas kernels, fused(): pl.pallas_call(functools.partial(kernel, nv, norb, nocc), out_shape=jax.S...  50.4 us
    unnamed x9, local copies, waits for them, and re-layouts  2.94 us

profile of v2, /device:TPU:4, one launch (start us, length us, event | category | flops | bytes accessed | tf_op | source)
XLA Modules:
  0.0 53.4 jit_solution(2397857107939128084)
XLA Ops:
  0.0 0.0 copy-start.2
  0.0 1.3 %copy.5.lad = bf16[640,320]{1,0:T(8,128)(2,1)S(1)} copy(bf16[640,320]{0,1:T(8,128)(2,1)} %param.5) | data formatting | bytes 819200 | tf_op args[1]
  1.3 0.0 copy-done.2
  1.3 0.0 copy-start
  1.3 0.0 copy-start.1
  1.4 0.3 copy.6.cyc
  1.6 0.7 %copy-done = bf16[200,640]{1,0:T(8,128)(2,1)S(1)} copy-done((bf16[200,640]{1,0:T(8,128)(2,1)S(1)}, bf16[200,640]{1,0:T(8,128)(2,1)}, u32[]{:S(2)}) %copy-start) | copy-done | bytes 256024
  2.3 0.0 copy-done.1
  2.3 50.4 %shard_map.46 = bf16[200,640]{1,0:T(8,128)(2,1)S(1)} custom-call(bf16[200,640]{1,0:T(8,128)(2,1)S(1)} %copy-done, bf16[640,320]{1,0:T(8,128)(2,1)S(1)} %copy.5.lad, bf16[640,320]{1,0:T(8,128)(2,1)S(1)} %copy.6.cyc, s32[5,10]{1,0:T(8,128)S(1)} %copy-done.1), custom_call_target="tpu_custom_call" | custom-call | tf_op jit(solution)/shard_map/pallas_call | solution.py:250
  52.7 0.7 %copy.8 = bf16[200,640]{1,0:T(8,128)(2,1)} copy(bf16[200,640]{1,0:T(8,128)(2,1)S(1)} %shard_map.46) | data formatting | bytes 512000
Async XLA Ops:
  0.0 1.3 %copy-start.2 = (bf16[640,320]{0,1:T(8,128)(2,1)S(1)}, bf16[640,320]{0,1:T(8,128)(2,1)}, u32[]{:S(2)}) copy-start(bf16[640,320]{0,1:T(8,128)(2,1)} %param.6) | copy-start | bytes 1228804
  1.3 1.0 %copy-start = (bf16[200,640]{1,0:T(8,128)(2,1)S(1)}, bf16[200,640]{1,0:T(8,128)(2,1)}, u32[]{:S(2)}) copy-start(bf16[200,640]{1,0:T(8,128)(2,1)} %amp.1) | copy-start | bytes 768004
  1.3 0.9 %copy-start.1 = (s32[5,10]{1,0:T(8,128)S(1)}, s32[5,10]{1,0:T(8,128)}, u32[]{:S(2)}) copy-start(s32[5,10]{1,0:T(8,128)} %scr.1) | copy-start | bytes 604

commit v3 on v2

v3 whole, which is shorter than its diff:
```python
import functools

import jax
import jax.numpy as jnp
from jax import lax
from jax.experimental import pallas as pl
from jax.experimental.pallas import tpu as pltpu
from jax.sharding import PartitionSpec as P

MESH = pl.DeviceIdType.MESH
LANES = 128
F32, BF16 = jnp.float32, jnp.bfloat16


def plain(amplitudes, ladder_ints, cycle_ints, screen):
    orbital_rows, tile_count = screen.shape
    occupied = amplitudes.shape[0] // orbital_rows
    columns = amplitudes.shape[1]
    tile_width = columns // tile_count
    groups = lax.axis_size("occ")
    values = screen.astype(F32)
    keep = jnp.broadcast_to(
        values[:, None, :, None], (orbital_rows, occupied, tile_count, tile_width)
    )
    keep = keep.reshape(orbital_rows * occupied, columns)
    masked = (amplitudes.astype(F32) * keep).astype(BF16)
    blocks = masked.reshape(orbital_rows, groups, orbital_rows, columns)
    arrived = lax.all_to_all(blocks, "occ", split_axis=1, concat_axis=1, tiled=True)
    swapped = arrived.transpose(2, 1, 0, 3).reshape(orbital_rows * occupied, columns)
    cycle_input = (2.0 * masked.astype(F32) - swapped.astype(F32)).astype(BF16)
    cycle_part = jnp.dot(
        cycle_input,
        lax.all_gather(cycle_ints, "occ", axis=1, tiled=True),
        preferred_element_type=F32,
    )
    ladder = jnp.dot(
        masked,
        lax.all_gather(ladder_ints, "occ", axis=1, tiled=True),
        preferred_element_type=F32,
    )
    summed = lax.psum_scatter(ladder + cycle_part, "vir", scatter_dimension=1, tiled=True)
    return (keep * summed).astype(BF16)


def ordinal(x, width, count):
    return sum((x >= width * n).astype(jnp.int32) for n in range(1, count))


def one_hot(target, width):
    lanes = lax.broadcasted_iota(jnp.int32, (target.shape[0], width), 1)
    return (lanes == target).astype(F32).astype(BF16)


def kernel(
    nv, norb, nocc,
    amp, lad, cyc, scr, out,
    G, I, W, O, T, R, F, keep_ref,
    gs, gr, osem, orx, lsem, lrx,
):
    rows, cols = out.shape
    groups, pad = G.shape[:2]
    half = cols // 2
    tile = cols // scr.shape[1]
    q4 = groups // 2
    jh = nocc // 2
    hr = rows // 2
    low = (hr // 16) * 16
    high = -(-hr // 16) * 16
    spans = ((0, low), (low, pad - low))
    gather = ((0, high), (high, pad - high))
    mid = -(-high // 32) * 16
    mid2 = high + -(-(pad - high) // 32) * 16
    subs = ((0, mid), (mid, high - mid), (high, mid2 - high), (mid2, pad - mid2))
    o = lax.axis_index("occ")
    z = lax.axis_index("vir")
    k = o % 2
    c = o // 2
    nc = nv
    sib = o + 1 - 2 * k
    cx = c + 1 - 2 * (c % 2)
    cy = c + 2 - 4 * ((c // 2) % 2)
    cd = cx + 2 - 4 * ((cx // 2) % 2)
    X, Y, D = 2 * cx + k, 2 * cy + k, 2 * cd + k

    barrier = pltpu.get_barrier_semaphore()
    for p in (sib, X, Y, D):
        pl.semaphore_signal(barrier, inc=1, device_id={"occ": p, "vir": z}, device_id_type=MESH)
    for there, ok in ((z - 1, z > 0), (z + 1, z < nv - 1)):

        @pl.when(ok)
        def _():
            pl.semaphore_signal(
                barrier, inc=1, device_id={"occ": o, "vir": there}, device_id_type=MESH
            )

    t_of = lax.broadcasted_iota(jnp.int32, (scr.shape[1], cols), 0)
    v_of = lax.broadcasted_iota(jnp.int32, (scr.shape[1], cols), 1)
    spread = ((v_of >= t_of * tile) & (v_of < (t_of + 1) * tile)).astype(F32)
    wide = jnp.dot(scr[...].astype(F32), spread, preferred_element_type=F32)
    r_of = lax.broadcasted_iota(jnp.int32, (rows, norb), 0)
    a_of = lax.broadcasted_iota(jnp.int32, (rows, norb), 1)
    pick = ((r_of >= a_of * nocc) & (r_of < (a_of + 1) * nocc)).astype(F32)
    keep = jnp.dot(pick, wide, preferred_element_type=F32)
    keep_ref[...] = keep
    masked = (amp[...].astype(F32) * keep).astype(BF16)

    side = o // q4
    r = lax.broadcasted_iota(jnp.int32, (pad, 1), 0)
    cl = ordinal(r, hr, 2)
    rr = r - cl * hr
    a = ordinal(rr, jh, norb)
    source = a * nocc + (cl + side - 2 * cl * side) * jh + rr - a * jh
    source = jnp.where(r < rows, source, -1)
    G[o] = jnp.dot(one_hot(source, rows), masked, preferred_element_type=F32).astype(BF16)

    pl.semaphore_wait(barrier, jnp.where((z == 0) | (z == nv - 1), 5, 6))

    def cp(src, dst, sem, p):
        return pltpu.make_async_remote_copy(
            src_ref=src, dst_ref=dst, send_sem=gs.at[sem], recv_sem=gr.at[sem],
            device_id={"occ": p, "vir": z}, device_id_type=MESH,
        )

    sends = []

    def send(s, span, sem, p):
        ref = G.at[s, pl.ds(*span)]
        d = cp(ref, ref, sem, p)
        d.start()
        sends.append(d)

    def arrive(s, span, sem):
        ref = G.at[s, pl.ds(*span)]
        cp(ref, ref, sem, sib).wait_recv()

    SX, SY, SD = X + 1 - 2 * k, Y + 1 - 2 * k, D + 1 - 2 * k

    def own_out(n):
        e, f = subs[2 * n], subs[2 * n + 1]
        b = 10 * n
        send(o, e, b + 0, X)
        send(o, f, b + 3, Y)
        send(o, f, b + 1, X)
        send(o, e, b + 2, Y)
        send(o, gather[n], b + 6, sib)

    def forward(n):
        e, f = subs[2 * n], subs[2 * n + 1]
        b = 10 * n
        arrive(X, e, b + 0)
        send(X, e, b + 4, Y)
        arrive(Y, f, b + 3)
        send(Y, f, b + 5, X)

    def collect(n):
        e, f = subs[2 * n], subs[2 * n + 1]
        b = 10 * n
        arrive(X, f, b + 1)
        send(X, gather[n], b + 7, sib)
        arrive(Y, e, b + 2)
        send(Y, gather[n], b + 8, sib)

    def finish(n):
        e, f = subs[2 * n], subs[2 * n + 1]
        b = 10 * n
        arrive(sib, gather[n], b + 6)
        arrive(D, e, b + 4)
        arrive(D, f, b + 5)
        send(D, gather[n], b + 9, sib)
        arrive(SX, gather[n], b + 7)
        arrive(SY, gather[n], b + 8)
        arrive(SD, gather[n], b + 9)

    own_out(0)
    for m, ref in enumerate((lad, cyc)):
        d = cp(ref, I.at[k, m], 20 + m, sib)
        d.start()
        sends.append(d)
        I[k, m] = ref[...]
    forward(0)
    own_out(1)
    collect(0)
    for m in range(2):
        cp(I.at[1 - k, m], I.at[1 - k, m], 20 + m, sib).wait_recv()
        W[m] = jnp.concatenate([I[0, m], I[1, m]], axis=1)
    finish(0)

    def out_copy(n, t, chip, slot):
        return pltpu.make_async_remote_copy(
            src_ref=O.at[t, pl.ds(*spans[n])], dst_ref=T.at[slot, pl.ds(*spans[n])],
            send_sem=osem.at[n, t], recv_sem=orx.at[n, slot],
            device_id={"occ": 2 * chip + k, "vir": z}, device_id_type=MESH,
        )

    def compute(n):
        at, size = spans[n]
        r = at + lax.broadcasted_iota(jnp.int32, (size, 1), 0)
        cl = ordinal(r, hr, 2)
        rr = r - cl * hr
        a = ordinal(rr, jh, norb)
        jj = rr - a * jh
        sd = ordinal(jj, norb, q4)
        row = (jj - sd * norb) * jh + a
        if n == 0:
            base = sd * high + row
            width = q4 * high
        else:
            base = jnp.where(cl == 0, q4 * size + row, sd * size + hr - at + row)
            base = jnp.where(r < rows, base, -groups * pad)
            width = q4 * size + high

        def step(t, carry):
            chip = (c + t + 1) % nc
            dest = 2 * chip + k
            there = dest // q4
            m = G[dest, pl.ds(at, size)]
            if n == 0:
                pool = [G[there * q4 + s, pl.ds(0, high)] for s in range(q4)]
            else:
                pool = [G[(1 - there) * q4 + s, pl.ds(at, size)] for s in range(q4)]
                pool.append(G[there * q4 + q4 - 1, pl.ds(0, high)])
            pool = jnp.concatenate(pool, axis=0)
            perm = one_hot(base + (dest % q4) * norb, width)
            swapped = jnp.dot(perm, pool, preferred_element_type=F32)
            ci = (2.0 * m.astype(F32) - swapped).astype(BF16)
            acc = jnp.dot(m, W[0], preferred_element_type=F32)
            acc = acc + jnp.dot(ci, W[1], preferred_element_type=F32)
            acc = acc.astype(BF16)

            @pl.when(t == nc - 1)
            def _():
                T[c, pl.ds(at, size)] = acc

            @pl.when(t < nc - 1)
            def _():
                O[t, pl.ds(at, size)] = acc
                out_copy(n, t, chip, c).start()

            return carry

        lax.fori_loop(0, nc, step, 0)

    forward(1)
    compute(0)
    collect(1)
    finish(1)
    compute(1)

    def line_copy(n, src, way, tile_at, there):
        return pltpu.make_async_remote_copy(
            src_ref=src.at[pl.ds(*spans[n])], dst_ref=R.at[way, tile_at, pl.ds(*spans[n])],
            send_sem=lsem.at[n, way, tile_at], recv_sem=lrx.at[n, way, tile_at],
            device_id={"occ": o, "vir": there}, device_id_type=MESH,
        )

    def plane_wait(n, at):
        @pl.when(c != at)
        def _():
            out_copy(n, 0, c, at).wait_recv()

    for zz in range(nv):

        @pl.when(z == zz)
        def _():
            ups = [(q, 0) for q in range(nv - 1, zz, -1)]
            downs = [(q, 1) for q in range(zz)]
            order = ups + downs if 2 * zz < nv else downs + ups
            started = []
            for n in range(2):
                span = pl.ds(*spans[n])
                for q, way in order:
                    there = zz + 1 if way == 0 else zz - 1
                    first = zz == 0 if way == 0 else zz == nv - 1
                    plane_wait(n, q)
                    if first:
                        src = T.at[q]
                    else:
                        src = R.at[way, q]
                        line_copy(n, src, way, q, there).wait_recv()
                        R[way, q, span] = (
                            R[way, q, span].astype(F32) + T[q, span].astype(F32)
                        ).astype(BF16)
                    d = line_copy(n, src, way, q, there)
                    d.start()
                    started.append(d)
            for n in range(2):
                span = pl.ds(*spans[n])
                plane_wait(n, zz)
                total = T[zz, span].astype(F32)
                for way, any_in in ((0, zz > 0), (1, zz < nv - 1)):
                    if any_in:
                        line_copy(
                            n, R.at[way, zz], way, zz, zz + 1 if zz == 0 else zz - 1
                        ).wait_recv()
                        total = total + R[way, zz, span].astype(F32)
                F[span] = total.astype(BF16)
            for d in started:
                d.wait_send()

    r = lax.broadcasted_iota(jnp.int32, (rows, 1), 0)
    a = ordinal(r, nocc, norb)
    j = r - a * nocc
    jside = ordinal(j, jh, 2)
    cl = jside + side - 2 * jside * side
    place = cl * hr + a * jh + j - jside * jh
    back = jnp.dot(one_hot(place, pad), F[...], preferred_element_type=F32)
    out[...] = (keep_ref[...] * back).astype(BF16)

    for d in sends:
        d.wait_send()
    for n in range(2):
        for t in range(nc - 1):
            out_copy(n, t, c, c).wait_send()


def fused(amplitudes, ladder_ints, cycle_ints, screen):
    norb, tiles = screen.shape
    rows, cols = amplitudes.shape
    nocc = rows // norb
    nv = lax.axis_size("vir")
    groups = lax.axis_size("occ")
    pad = -(-rows // 16) * 16
    vmem = pl.BlockSpec(memory_space=pltpu.VMEM)
    return pl.pallas_call(
        functools.partial(kernel, nv, norb, nocc),
        out_shape=jax.ShapeDtypeStruct((rows, cols), BF16),
        in_specs=[vmem] * 4,
        out_specs=vmem,
        scratch_shapes=[
            pltpu.VMEM((groups, pad, cols), BF16),
            pltpu.VMEM((2, 2) + ladder_ints.shape, BF16),
            pltpu.VMEM((2, cols, cols), BF16),
            pltpu.VMEM((nv - 1, pad, cols), BF16),
            pltpu.VMEM((nv, pad, cols), BF16),
            pltpu.VMEM((2, nv, pad, cols), BF16),
            pltpu.VMEM((pad, cols), BF16),
            pltpu.VMEM((rows, cols), F32),
            pltpu.SemaphoreType.DMA((22,)),
            pltpu.SemaphoreType.DMA((22,)),
            pltpu.SemaphoreType.DMA((2, nv - 1)),
            pltpu.SemaphoreType.DMA((2, nv)),
            pltpu.SemaphoreType.DMA((2, 2, nv)),
            pltpu.SemaphoreType.DMA((2, 2, nv)),
        ],
        compiler_params=pltpu.CompilerParams(
            collective_id=0, has_side_effects=True, vmem_limit_bytes=48 * 2**20
        ),
    )(amplitudes, ladder_ints, cycle_ints, screen)


def shards(amplitudes, ladder_ints, cycle_ints, screen):
    groups, planes = lax.axis_size("occ"), lax.axis_size("vir")
    rows, cols = amplitudes.shape
    fits = (
        groups == 2 * planes
        and planes == 4
        and cols == 2 * ladder_ints.shape[1]
        and cols == ladder_ints.shape[0]
        and cols % LANES == 0
        and rows % 16 == 8
        and rows // screen.shape[0] == groups * screen.shape[0]
        and (rows // 2) % 16 <= screen.shape[0]
        and groups * rows * cols * 2 < 16 * 2**20
    )
    return (fused if fits else plain)(amplitudes, ladder_ints, cycle_ints, screen)


def solution(mesh):
    placed = (P("occ", "vir"), P("vir", "occ"), P("vir", "occ"), P("occ", "vir"))
    return jax.shard_map(
        shards, mesh=mesh, in_specs=placed, out_specs=P("occ", "vir"), check_vma=False
    )
```

time: 53.5 us -> 47.8 us (0.89)
  the two profiles are of different devices: /device:TPU:4 before, /device:TPU:0 now
where the time goes in v3:
time: 47.8 us; the launch traced here: 47.6 us
  Pallas kernels  44.6 us (93%)
  local copies, waits for them, and re-layouts  2.94 us (6%)
    pallas_call x1, Pallas kernels, fused(): pl.pallas_call(functools.partial(kernel, nv, norb, nocc), out_shape=jax.S...  44.6 us
    unnamed x9, local copies, waits for them, and re-layouts  2.94 us

profile of v3, /device:TPU:0, one launch (start us, length us, event | category | flops | bytes accessed | tf_op | source)
XLA Modules:
  0.0 47.6 jit_solution(15918332914049332401)
XLA Ops:
  0.0 0.0 copy-start.2
  0.0 1.3 %copy.5.lad = bf16[640,320]{1,0:T(8,128)(2,1)S(1)} copy(bf16[640,320]{0,1:T(8,128)(2,1)} %param.5) | data formatting | bytes 819200 | tf_op args[1]
  1.3 0.0 copy-done.2
  1.3 0.0 copy-start
  1.3 0.0 copy-start.1
  1.4 0.3 copy.6.cyc
  1.6 0.7 %copy-done = bf16[200,640]{1,0:T(8,128)(2,1)S(1)} copy-done((bf16[200,640]{1,0:T(8,128)(2,1)S(1)}, bf16[200,640]{1,0:T(8,128)(2,1)}, u32[]{:S(2)}) %copy-start) | copy-done | bytes 256024
  2.3 0.0 copy-done.1
  2.3 44.6 %shard_map.46 = bf16[200,640]{1,0:T(8,128)(2,1)S(1)} custom-call(bf16[200,640]{1,0:T(8,128)(2,1)S(1)} %copy-done, bf16[640,320]{1,0:T(8,128)(2,1)S(1)} %copy.5.lad, bf16[640,320]{1,0:T(8,128)(2,1)S(1)} %copy.6.cyc, s32[5,10]{1,0:T(8,128)S(1)} %copy-done.1), custom_call_target="tpu_custom_call" | custom-call | tf_op jit(solution)/shard_map/pallas_call | solution.py:324
  46.9 0.7 %copy.8 = bf16[200,640]{1,0:T(8,128)(2,1)} copy(bf16[200,640]{1,0:T(8,128)(2,1)S(1)} %shard_map.46) | data formatting | bytes 512000
Async XLA Ops:
  0.0 1.3 %copy-start.2 = (bf16[640,320]{0,1:T(8,128)(2,1)S(1)}, bf16[640,320]{0,1:T(8,128)(2,1)}, u32[]{:S(2)}) copy-start(bf16[640,320]{0,1:T(8,128)(2,1)} %param.6) | copy-start | bytes 1228804
  1.3 1.0 %copy-start = (bf16[200,640]{1,0:T(8,128)(2,1)S(1)}, bf16[200,640]{1,0:T(8,128)(2,1)}, u32[]{:S(2)}) copy-start(bf16[200,640]{1,0:T(8,128)(2,1)} %amp.1) | copy-start | bytes 768004
  1.3 0.9 %copy-start.1 = (s32[5,10]{1,0:T(8,128)S(1)}, s32[5,10]{1,0:T(8,128)}, u32[]{:S(2)}) copy-start(s32[5,10]{1,0:T(8,128)} %scr.1) | copy-start | bytes 604
